TPU v7x, 256 devices: a whole 4x4x8 slice. The times are simulated.
256 devices in a mesh: dp: 2 (over y_lo), expert: 8 (over x, y_hi), etp: 16 (over z, core).
Axes of the slice: x: 4, y: 4 (y_hi: 2, y_lo: 2; y = y_hi * 2 + y_lo), z: 8, core: 2. Of those that a mesh axis runs over, the one named last changes fastest.
Arguments:
- tokens: bfloat16 [2048, 6144], P(('dp', 'expert'), 'etp'), may hold values from -6 to 6
- routes: int32 [2048, 2], P(('dp', 'expert')), may hold values from 0 to 7, all different within a row; in each aligned block of 128 rows (0 to 127, 128 to 255, ...) at most 48 rows name the same one
- w_gate: bfloat16 [8, 6144, 8192], P('expert', 'dp', 'etp'), may hold values from -0.078125 to 0.078125
- w_up: bfloat16 [8, 6144, 8192], P('expert', 'dp', 'etp'), may hold values from -0.078125 to 0.078125
- slot_grad: bfloat16 [2, 8, 8, 48, 8192], P('dp', 'expert', None, None, 'etp'), may hold values from -1.5 to 1.5
Outputs:
- token_grad: bfloat16 [2048, 6144], P(('dp', 'expert'), 'etp')
- gate_grad: bfloat16 [8, 6144, 8192], P('expert', 'dp', 'etp')
- up_grad: bfloat16 [8, 6144, 8192], P('expert', 'dp', 'etp')
Inputs may be any that keep to these rules, and one draw needn't show every extreme that they name: `routes`: each token names 2 different experts. Among the tokens of one source no expert is named more than 48 times, and in every draw the tokens of some source name some expert exactly 48 times.
All inputs are finite; a program needn't handle non-finite values.
Results may differ from a plain program's by a relative error of at most 0.025.
Values may be sent and summed in bfloat16 or wider, within the bound.
A program may use at most 128 MiB of HBM per device.

v0:
```python
import jax
import jax.numpy as jnp
from jax import lax
from jax.sharding import PartitionSpec as P


def local(tokens, routes, w_gate, w_up, slot_grad):
    tok_dev = tokens.shape[0]
    experts = lax.axis_size("expert")
    cap = slot_grad.shape[3]
    hidden = w_gate.shape[2]
    pairs = routes.reshape(-1)
    onehot = (pairs[:, None] == jnp.arange(experts, dtype=jnp.int32)[None, :]).astype(jnp.int32)
    before = jnp.cumsum(onehot, axis=0) - onehot
    slot = jnp.sum(before * onehot, axis=1)
    target = pairs * cap + slot
    place = (target[:, None] == jnp.arange(experts * cap, dtype=jnp.int32)[None, :]).astype(
        jnp.bfloat16
    )
    token_of = place.reshape(tok_dev, routes.shape[1], experts * cap).sum(axis=1)
    outgoing = lax.dot_general(
        token_of, tokens, (((0,), (0,)), ((), ())), preferred_element_type=jnp.float32
    )
    outgoing = outgoing.astype(jnp.bfloat16).reshape(experts, cap, tokens.shape[1])
    arrived = lax.all_to_all(outgoing, "expert", split_axis=0, concat_axis=0, tiled=True)
    gathered = lax.all_gather(arrived, "etp", axis=2, tiled=True)
    width = gathered.shape[2]
    row_count = gathered.shape[0] * cap
    x_rows = gathered.reshape(row_count, width)
    grad_rows = slot_grad[0, 0].reshape(row_count, hidden).astype(jnp.float32)
    joined = jnp.concatenate((w_gate[0], w_up[0]), axis=1)
    full = lax.all_gather(joined, "dp", axis=0, tiled=True)
    both = jnp.dot(x_rows, full, preferred_element_type=jnp.float32)
    gate = both[:, :hidden]
    up = both[:, hidden:]
    sig = jax.nn.sigmoid(gate)
    d_gate = (grad_rows * up * sig * (1.0 + gate * (1.0 - sig))).astype(jnp.bfloat16)
    d_up = (grad_rows * gate * sig).astype(jnp.bfloat16)
    d_both = jnp.concatenate((d_gate, d_up), axis=1)
    summed_weights = lax.psum_scatter(
        lax.dot_general(
            x_rows, d_both, (((0,), (0,)), ((), ())), preferred_element_type=jnp.float32
        ).astype(jnp.bfloat16),
        "dp",
        scatter_dimension=0,
        tiled=True,
    )
    gate_grad = summed_weights[:, :hidden][None]
    up_grad = summed_weights[:, hidden:][None]
    summed = lax.psum_scatter(
        lax.dot_general(
            full, d_both, (((1,), (1,)), ((), ())), preferred_element_type=jnp.float32
        ).astype(jnp.bfloat16),
        "etp",
        scatter_dimension=0,
        tiled=True,
    ).astype(jnp.float32)
    back = summed.astype(jnp.bfloat16).reshape(summed.shape[0], experts, cap)
    returned = lax.all_to_all(back, "expert", split_axis=1, concat_axis=1, tiled=True)
    returned = returned.reshape(summed.shape[0], experts * cap)
    token_grad = lax.dot_general(
        token_of, returned, (((1,), (1,)), ((), ())), preferred_element_type=jnp.float32
    )
    return (token_grad.astype(jnp.bfloat16), gate_grad, up_grad)


def solution(mesh):
    in_specs = (
        P(("dp", "expert"), "etp"),
        P(("dp", "expert"), None),
        P("expert", "dp", "etp"),
        P("expert", "dp", "etp"),
        P("dp", "expert", None, None, "etp"),
    )
    out_specs = (P(("dp", "expert"), "etp"), P("expert", "dp", "etp"), P("expert", "dp", "etp"))
    return jax.shard_map(local, mesh=mesh, in_specs=in_specs, out_specs=out_specs, check_vma=False)
```

profile of v0, /device:TPU:32, one launch (start us, length us, event | category | flops | bytes accessed | tf_op | source)
XLA Modules:
  0.0 473.0 jit_solution(14712970462131785293)
XLA Ops:
  7.2 0.0 copy-start
  7.2 0.0 all-gather.5.cloned.1.call-start
  7.2 0.8 copy.20
  8.0 0.1 eq.43
  8.2 0.1 eq.39
  8.3 0.6 reduce-window.6
  8.9 0.2 slice_reduce_fusion
  9.1 0.1 fusion.8
  9.2 0.1 reduce_sum.24
  9.4 0.1 copy.22
  9.5 0.7 multiply_add_fusion
  10.2 0.1 fusion.6
  10.3 0.0 copy-done
  10.3 0.3 convolution_convert_fusion.2
  10.5 16.1 %all_to_all.10 = bf16[8,48,384]{2,1,0:T(8,128)(2,1)} all-to-all(bf16[8,48,384]{2,1,0:T(8,128)(2,1)S(1)} %bitcast.34), channel_id=1, replica_groups=mesh['dp'=2,'expert'=8,'etp'=16] {'expert'}, dimensions={0} | all-to-all | bytes 589824 | tf_op jit(solution)/shard_map/all_to_all | solution.py:25
  26.7 0.0 all-gather.5.cloned.1.call-update
  26.7 0.0 all-gather.3.cloned.1.call-start
  26.7 6.3 %pad_maximum_fusion = bf16[3072,1024]{1,0:T(8,128)(2,1)} fusion(bf16[3072,512]{1,0:T(8,128)(2,1)} %bitcast.30, bf16[3072,512]{1,0:T(8,128)(2,1)} %bitcast.31), kind=kLoop, calls=%fused_computation.2 | loop fusion | flops 12582912 | bytes 12582912 | tf_op jit(solution)/shard_map/concatenate | solution.py:31
  33.1 0.0 all-gather.3.cloned.1.call-update
  33.1 0.0 reduce-scatter.3.cloned.1.call-start
  33.1 35.0 %all-gather.5.cloned.1.call-done = bf16[8,48,6144]{2,1,0:T(8,128)(2,1)} async-done(((bf16[8,48,384]{2,1,0:T(8,128)(2,1)}), bf16[8,48,6144]{2,1,0:T(8,128)(2,1)}) %all-gather.5.cloned.1.call-update) | async-done | bytes 4718608 | tf_op jit(solution)/shard_map/all_gather | solution.py:26
  68.2 158.5 %all-gather.3.cloned.1.call-done = bf16[6144,1024]{1,0:T(8,128)(2,1)} async-done(((bf16[3072,1024]{1,0:T(8,128)(2,1)}), bf16[6144,1024]{1,0:T(8,128)(2,1)}) %all-gather.3.cloned.1.call-update) | async-done | bytes 12582928 | tf_op jit(solution)/shard_map/all_gather | solution.py:32
  226.7 0.0 copy-start.1
  226.7 0.0 copy-start.2
  226.7 9.5 %fusion.12 = f32[384,1024]{1,0:T(8,128)S(1)} fusion(bf16[384,6144]{1,0:T(8,128)(2,1)} %bitcast.35, bf16[6144,1024]{1,0:T(8,128)(2,1)} %all-gather.3.cloned.1.call-done), kind=kOutput, calls=%fused_computation.29 | convolution fusion | flops 4831838208 | bytes 18874368 | tf_op jit(solution)/shard_map/dot_general | solution.py:33
  236.2 0.0 copy-done.1
  236.2 0.4 fusion.2
  236.6 0.0 copy-done.2
  236.6 8.5 %convolution_convert_fusion.1 = bf16[6144,384]{1,0:T(8,128)(2,1)} fusion(bf16[6144,1024]{1,0:T(8,128)(2,1)S(1)} %copy-done.2, bf16[384,512]{1,0:T(8,128)(2,1)S(1)} %get-tuple-element.6, bf16[384,512]{1,0:T(8,128)(2,1)S(1)} %get-tuple-element.5), kind=kOutput, calls=%fused_computation.1 | convolution fusion | flops 4835770368 | bytes 18087936 | tf_op jit(solution)/shard_map/dot_general | solution.py:51
  245.1 0.0 reduce-scatter.3.cloned.1.call-update
  245.1 0.0 reduce-scatter.5.cloned.1.call-start
  245.2 12.2 %convolution_convert_fusion = bf16[6144,1024]{1,0:T(8,128)(2,1)} fusion(bf16[384,6144]{1,0:T(8,128)(2,1)} %bitcast.36, bf16[384,512]{1,0:T(8,128)(2,1)S(1)} %get-tuple-element.6, bf16[384,512]{1,0:T(8,128)(2,1)S(1)} %get-tuple-element.5), kind=kOutput, calls=%fused_computation | convolution fusion | flops 4839702528 | bytes 18087936 | tf_op jit(solution)/shard_map/dot_general | solution.py:41
  257.4 0.0 reduce-scatter.5.cloned.1.call-update
  257.4 49.2 %reduce-scatter.3.cloned.1.call-done = bf16[384,384]{1,0:T(8,128)(2,1)} async-done(((bf16[6144,384]{1,0:T(8,128)(2,1)}), bf16[384,384]{1,0:T(8,128)(2,1)}) %reduce-scatter.3.cloned.1.call-update) | async-done | bytes 294928 | tf_op jit(solution)/shard_map/reduce_scatter | solution.py:50
  306.6 1.2 copy.23
  307.8 15.6 %all_to_all.11 = bf16[384,8,48]{0,2,1:T(8,128)(2,1)S(1)} all-to-all(bf16[384,8,48]{0,2,1:T(8,128)(2,1)S(1)} %bitcast.32), channel_id=1, replica_groups=mesh['dp'=2,'expert'=8,'etp'=16] {'expert'}, dimensions={1} | all-to-all | bytes 589824 | tf_op jit(solution)/shard_map/all_to_all | solution.py:59
  323.3 0.9 convolution_convert_fusion.3
  324.2 136.4 %reduce-scatter.5.cloned.1.call-done = bf16[3072,1024]{1,0:T(8,128)(2,1)} async-done(((bf16[6144,1024]{1,0:T(8,128)(2,1)}), bf16[3072,1024]{1,0:T(8,128)(2,1)}) %reduce-scatter.5.cloned.1.call-update) | async-done | bytes 6291472 | tf_op jit(solution)/shard_map/reduce_scatter | solution.py:40
  460.6 5.9 %slice_bitcast_fusion = (bf16[1,3072,512]{2,1,0:T(8,128)(2,1)}, bf16[1,3072,512]{2,1,0:T(8,128)(2,1)}) fusion(bf16[3072,1024]{1,0:T(8,128)(2,1)} %reduce-scatter.5.cloned.1.call-done), kind=kLoop, calls=%fused_computation.3 | loop fusion | bytes 12582912 | tf_op jit(solution)/shard_map/broadcast_in_dim | solution.py:49
  (3 shorter events, 0.0 us)
Async XLA Ops:
  7.2 3.1 copy-start
  7.2 61.0 %all-gather.5.cloned.1.call-start = ((), (), s32[]{:S(2)}) async-start(), calls=%async_computation.5 | async-start | bytes 5013504 | tf_op jit(solution)/shard_map/all_gather | solution.py:26
  26.7 200.0 %all-gather.3.cloned.1.call-start = ((), (), s32[]{:S(2)}) async-start(), calls=%async_computation.4 | async-start | bytes 18874368 | tf_op jit(solution)/shard_map/all_gather | solution.py:32
  33.1 273.5 %reduce-scatter.3.cloned.1.call-start = ((), (), s32[]{:S(2)}) async-start(), calls=%async_computation.6 | async-start | bytes 5013504 | tf_op jit(solution)/shard_map/reduce_scatter | solution.py:50
  226.7 9.5 %copy-start.1 = (bf16[1,1,8,48,512]{4,3,2,1,0:T(8,128)(2,1)S(1)}, bf16[1,1,8,48,512]{4,3,2,1,0:T(8,128)(2,1)}, u32[]{:S(2)}) copy-start(bf16[1,1,8,48,512]{4,3,2,1,0:T(8,128)(2,1)} %param.9) | copy-start | bytes 1179652
  226.7 10.0 %copy-start.2 = (bf16[6144,1024]{1,0:T(8,128)(2,1)S(1)}, bf16[6144,1024]{1,0:T(8,128)(2,1)}, u32[]{:S(2)}) copy-start(bf16[6144,1024]{1,0:T(8,128)(2,1)} %all-gather.3.cloned.1.call-done) | copy-start | bytes 37748740
  245.1 215.4 %reduce-scatter.5.cloned.1.call-start = ((), (), s32[]{:S(2)}) async-start(), calls=%async_computation.7 | async-start | bytes 18874368 | tf_op jit(solution)/shard_map/reduce_scatter | solution.py:40
Sparse Core Ops, SparseCore 0:
  26.8 41.2 all-gather.4
  70.0 156.6 all-gather.2
  245.2 61.3 reduce-scatter.2
  309.0 151.5 reduce-scatter.4
where the time goes:
time: 475 us; the launch traced here: 473 us
  waiting for transfers between devices  379 us (80%)
  blocking collectives  31.7 us (7%)
  matrix products  31.3 us (7%)
  between operations  13.9 us (3%)
  local copies, waits for them, and re-layouts  8.61 us (2%)
  other arithmetic  8.28 us (2%)
    all_gather x1, waiting for transfers between devices, local(): full = lax.all_gather(joined, 'dp', axis=0, tiled=True)  158 us
    reduce_scatter x1, waiting for transfers between devices, local(): lax.psum_scatter(lax.dot_general(x_rows, d_both, (((0,), (0,)), ((), ()))...  136 us
    reduce_scatter x1, waiting for transfers between devices, local(): lax.psum_scatter(lax.dot_general(full, d_both, (((1,), (1,)), ((), ())),...  49.2 us
    all_gather x1, waiting for transfers between devices, local(): gathered = lax.all_gather(arrived, 'etp', axis=2, tiled=True)  35 us
    all_to_all x1, blocking collectives, local(): lax.all_to_all(outgoing, 'expert', split_axis=0, concat_axis=0, tiled=True)  16.1 us
    all_to_all x1, blocking collectives, local(): lax.all_to_all(back, 'expert', split_axis=1, concat_axis=1, tiled=True)  15.6 us
    dot_general x1, matrix products, local(): lax.dot_general(x_rows, d_both, (((0,), (0,)), ((), ())), preferred_eleme...  12.2 us
    dot_general x1, matrix products, local(): both = jnp.dot(x_rows, full, preferred_element_type=jnp.float32)  9.52 us
  transfers between devices with their start and end apart: 4, of which 4 were waited for; matrix products, arithmetic and copies ran while one was open for 4% of the time, Pallas kernels for 0%

commit v1 on v0

v1 whole, which is shorter than its diff:
```python
import functools

import jax
import jax.numpy as jnp
from jax import lax
from jax.experimental import pallas as pl
from jax.experimental.pallas import tpu as pltpu
from jax.sharding import PartitionSpec as P

MESH = pl.DeviceIdType.MESH
F32 = jnp.float32
BF16 = jnp.bfloat16

TAU = 2
LAG_Y1 = 2
LAG_Y2 = 2
LAG_RS = 1


def tile_of(size, most):
    return most if size % most == 0 else size


def kernel(
    outgoing, w_gate, w_up, slot_grad, token_of,
    token_grad, gate_grad, up_grad,
    w_v, rows, part, y_out, y_in, d_v, g_v, g_in, rs_out, rs_in, fin, ret, dw_v,
    w_sem, dw_sem, disp_send, disp_recv, ag_send, ag_recv, sib_send, sib_recv,
    y1_send, y1_recv, y2_send, y2_recv, g_send, g_recv, rs_send, rs_recv, ret_send, ret_recv,
):
    experts, cap, feat = outgoing.shape
    depth, hidden = w_gate.shape
    chips = depth // feat
    half = chips // 2
    r = lax.axis_index("dp")
    x = lax.axis_index("expert")
    m = lax.axis_index("etp")
    z = m // 2
    c = m % 2
    base = r * half
    home = z // half
    own = home == r
    zi = z - base
    sibling = (r, x, z * 2 + 1 - c)
    partner = (1 - r, x, m)
    ring = (
        (r, x, ((z + 1) % chips) * 2 + c),
        (r, x, ((z + chips - 1) % chips) * 2 + c),
    )

    def local_wait(ref, sem):
        pltpu.make_async_copy(ref, ref, sem).wait()

    def send(src, dst, send_sem, recv_sem, device):
        pltpu.make_async_remote_copy(
            src_ref=src, dst_ref=dst, send_sem=send_sem, recv_sem=recv_sem,
            device_id=device, device_id_type=MESH,
        ).start()

    load_gate = pltpu.make_async_copy(w_gate, w_v.at[:, pl.ds(0, hidden)], w_sem.at[0])
    load_up = pltpu.make_async_copy(w_up, w_v.at[:, pl.ds(hidden, hidden)], w_sem.at[1])
    load_gate.start()
    load_up.start()

    barrier = pltpu.get_barrier_semaphore()
    for device in ring + (sibling, partner):
        pl.semaphore_signal(barrier, inc=1, device_id=device, device_id_type=MESH)

    def greet(step, carry):
        there = (x + step) % experts
        for rr in range(2):
            pl.semaphore_signal(barrier, inc=1, device_id=(rr, there, m), device_id_type=MESH)
        return carry

    lax.fori_loop(1, experts, greet, 0)
    pl.semaphore_wait(barrier, 2 * (experts - 1) + 4)

    home_block = pl.ds(pl.multiple_of((m - home * chips) * feat, 128), feat)

    def dispatch(k, carry):
        there = (x + experts - k) % experts
        dst = rows.at[k, pl.ds(pl.multiple_of(r * cap, 16), cap), home_block]
        to_self = jnp.logical_and(own, k == 0)

        @pl.when(to_self)
        def _():
            pltpu.make_async_copy(outgoing.at[there], dst, disp_recv.at[k, r]).start()

        @pl.when(jnp.logical_not(to_self))
        def _():
            send(outgoing.at[there], dst, disp_send, disp_recv.at[k, r], (home, there, m))

        return carry

    lax.fori_loop(0, experts, dispatch, 0)

    def gather_hop(k, d, sub):
        source = (z + chips - d) % chips if sub == 0 else (z + d) % chips
        i = source - base

        @pl.when(jnp.logical_and(i >= 0, i < half))
        def _():
            block = rows.at[
                k, pl.ds(sub * cap, cap), pl.ds(pl.multiple_of((2 * i + c) * feat, 128), feat)
            ]

            @pl.when(d == 0)
            def _():
                local_wait(block, disp_recv.at[k, sub])

            @pl.when(d > 0)
            def _():
                local_wait(block, ag_recv.at[k, sub, i])

            @pl.when(d < chips - 1)
            def _():
                send(block, block, ag_send.at[sub], ag_recv.at[k, sub, i], ring[sub])

            send(block, block, sib_send, sib_recv.at[k], sibling)

    def reduce_hop(k, d, sub):
        target = (z + 2 * chips - 1 - d) % chips if sub == 0 else (z + 1 + d) % chips
        i = target - base

        @pl.when(jnp.logical_and(i >= 0, i < half))
        def _():
            here = pl.ds(sub * cap, cap)
            column = pl.ds(pl.multiple_of((2 * i + c) * feat, 128), feat)
            packed = pl.ds(pl.multiple_of(i * feat, 128), feat)
            total = g_v[k, here, column].astype(F32) + g_in[k, here, packed].astype(F32)

            @pl.when(d == 0)
            def _():
                rs_out[k, sub, i] = total.astype(BF16)

            @pl.when(d > 0)
            def _():
                local_wait(rs_in.at[k, sub, i], rs_recv.at[k, sub, i])
                rs_out[k, sub, i] = (total + rs_in[k, sub, i].astype(F32)).astype(BF16)

            @pl.when(d < chips - 1)
            def _():
                send(
                    rs_out.at[k, sub, i], rs_in.at[k, sub, i],
                    rs_send, rs_recv.at[k, sub, i], ring[sub],
                )

            @pl.when(d == chips - 1)
            def _():
                there = (x + k) % experts
                to_self = jnp.logical_and(r == sub, k == 0)

                @pl.when(to_self)
                def _():
                    pltpu.make_async_copy(rs_out.at[k, sub, i], ret.at[x], ret_recv.at[x]).start()

                @pl.when(jnp.logical_not(to_self))
                def _():
                    send(rs_out.at[k, sub, i], ret.at[x], ret_send, ret_recv.at[x], (sub, there, m))

    mine = pl.ds(pl.multiple_of(r * cap, 16), cap)
    other = pl.ds(pl.multiple_of((1 - r) * cap, 16), cap)
    wide = 2 * hidden
    fwd_tile = tile_of(wide, 256)
    dx_tile = tile_of(depth, 256)

    def forward(k):
        @pl.when(k == 0)
        def _():
            load_gate.wait()
            load_up.wait()

        local_wait(rows.at[k, :, pl.ds(0, half * feat)], sib_recv.at[k])

        def tile(j, carry):
            columns = pl.ds(pl.multiple_of(j * fwd_tile, 128), fwd_tile)
            part[k, :, columns] = jnp.dot(rows[k], w_v[:, columns], preferred_element_type=F32)
            return carry

        lax.fori_loop(0, wide // fwd_tile, tile, 0)
        y_out[k] = part[k, other, :].astype(BF16)
        send(y_out.at[k], y_in.at[k], y1_send, y1_recv.at[k], partner)

    def activate(k):
        local_wait(y_in.at[k], y1_recv.at[k])
        gate = part[k, mine, pl.ds(0, hidden)] + y_in[k, :, pl.ds(0, hidden)].astype(F32)
        up = part[k, mine, pl.ds(hidden, hidden)] + y_in[k, :, pl.ds(hidden, hidden)].astype(F32)
        g = slot_grad[(x + k) % experts].astype(F32)
        sig = jax.nn.sigmoid(gate)
        gs = g * sig
        d_v[k, mine, pl.ds(0, hidden)] = (gs * up * (1.0 + gate * (1.0 - sig))).astype(BF16)
        d_v[k, mine, pl.ds(hidden, hidden)] = (gs * gate).astype(BF16)
        send(d_v.at[k, mine, :], d_v.at[k, mine, :], y2_send, y2_recv.at[k], partner)

    def backward(k):
        local_wait(d_v.at[k, other, :], y2_recv.at[k])

        def tile(j, carry):
            columns = pl.ds(pl.multiple_of(j * dx_tile, 128), dx_tile)
            g_v[k, :, columns] = lax.dot_general(
                d_v[k], w_v[columns, :], (((1,), (1,)), ((), ())), preferred_element_type=F32
            ).astype(BF16)
            return carry

        lax.fori_loop(0, depth // dx_tile, tile, 0)
        for i in range(half):
            column = pl.ds(pl.multiple_of((2 * i + 1 - c) * feat, 128), feat)
            send(
                g_v.at[k, :, column], g_in.at[k, :, pl.ds(i * feat, feat)],
                g_send, g_recv.at[k], sibling,
            )

    dw_tile = tile_of(hidden, 256)

    def weight_piece(p):
        feats = pl.ds(pl.multiple_of(p * feat, 128), feat)
        block = rows[:, :, feats].reshape(experts * 2 * cap, feat)

        def tile(j, carry):
            columns = pl.ds(pl.multiple_of(j * dw_tile, 128), dw_tile)
            dw_v[feats, columns] = lax.dot_general(
                block, d_v[:, :, columns].reshape(experts * 2 * cap, dw_tile),
                (((0,), (0,)), ((), ())), preferred_element_type=F32,
            ).astype(BF16)
            return carry

        lax.fori_loop(0, wide // dw_tile, tile, 0)
        pltpu.make_async_copy(
            dw_v.at[feats, pl.ds(0, hidden)], gate_grad.at[feats, :], dw_sem.at[p, 0]
        ).start()
        pltpu.make_async_copy(
            dw_v.at[feats, pl.ds(hidden, hidden)], up_grad.at[feats, :], dw_sem.at[p, 1]
        ).start()

    at_fwd = chips
    at_y1 = at_fwd + LAG_Y1
    at_y2 = at_y1 + LAG_Y2
    at_rs = at_y2 + LAG_RS
    last = TAU * (experts - 1)
    ticks = last + at_rs + chips
    at_dw = last + at_y2 + 1

    def tick(t, carry):
        def transfers(k, inner):
            u = t - TAU * k
            d = u - at_rs

            @pl.when(d == 0)
            def _():
                local_wait(g_in.at[k], g_recv.at[k])

            @pl.when(jnp.logical_and(d >= 0, d < chips))
            def _():
                reduce_hop(k, d, 0)
                reduce_hop(k, d, 1)

            @pl.when(jnp.logical_and(u >= 0, u < chips))
            def _():
                gather_hop(k, u, 0)
                gather_hop(k, u, 1)

            return inner

        lax.fori_loop(0, experts, transfers, 0)

        def work(k, inner):
            u = t - TAU * k
            pl.when(u == at_y1)(functools.partial(activate, k))
            pl.when(u == at_y2)(functools.partial(backward, k))
            pl.when(u == at_fwd)(functools.partial(forward, k))
            return inner

        lax.fori_loop(0, experts, work, 0)
        p = t - at_dw
        pl.when(jnp.logical_and(p >= 0, p < chips))(functools.partial(weight_piece, p))
        return carry

    lax.fori_loop(0, ticks, tick, 0)

    def late_piece(p, carry):
        weight_piece(p)
        return carry

    lax.fori_loop(max(0, ticks - at_dw), chips, late_piece, 0)

    def returned(k, carry):
        local_wait(ret.at[k], ret_recv.at[k])
        return carry

    lax.fori_loop(0, experts, returned, 0)
    token_grad[...] = jnp.dot(
        token_of[...], ret[...].reshape(experts * cap, feat), preferred_element_type=F32
    ).astype(BF16)

    @pl.when(own)
    def _():
        local_wait(outgoing.at[pl.ds(0, experts - 1)], disp_send)
        local_wait(fin, ret_send)
        local_wait(rs_out.at[:, :, pl.ds(0, half - 1)], rs_send)

    @pl.when(jnp.logical_not(own))
    def _():
        local_wait(outgoing, disp_send)
        local_wait(rs_out, rs_send)

    for sub, after in ((0, (z + 1) % chips), (1, (z + chips - 1) % chips)):
        inside = after // half == r

        @pl.when(inside)
        def _():
            local_wait(rows.at[:, pl.ds(0, cap), pl.ds(0, (half - 1) * feat)], ag_send.at[sub])

        @pl.when(jnp.logical_not(inside))
        def _():
            local_wait(rows.at[:, pl.ds(0, cap), pl.ds(0, half * feat)], ag_send.at[sub])

    local_wait(rows.at[:, :, pl.ds(0, half * feat)], sib_send)
    local_wait(y_out, y1_send)
    local_wait(d_v.at[:, pl.ds(0, cap), :], y2_send)
    local_wait(g_in, g_send)

    def written(p, carry):
        feats = pl.ds(pl.multiple_of(p * feat, 128), feat)
        local_wait(dw_v.at[feats, pl.ds(0, hidden)], dw_sem.at[p, 0])
        local_wait(dw_v.at[feats, pl.ds(hidden, hidden)], dw_sem.at[p, 1])
        return carry

    lax.fori_loop(0, chips, written, 0)


def local(tokens, routes, w_gate, w_up, slot_grad):
    tok_dev, feat = tokens.shape
    experts = lax.axis_size("expert")
    cap = slot_grad.shape[3]
    _, depth, hidden = w_gate.shape
    half = depth // feat // 2
    pairs = routes.reshape(-1)
    onehot = (pairs[:, None] == jnp.arange(experts, dtype=jnp.int32)[None, :]).astype(jnp.int32)
    before = jnp.cumsum(onehot, axis=0) - onehot
    slot = jnp.sum(before * onehot, axis=1)
    target = pairs * cap + slot
    place = (target[:, None] == jnp.arange(experts * cap, dtype=jnp.int32)[None, :]).astype(BF16)
    token_of = place.reshape(tok_dev, routes.shape[1], experts * cap).sum(axis=1)
    outgoing = lax.dot_general(
        token_of, tokens, (((0,), (0,)), ((), ())), preferred_element_type=F32
    )
    outgoing = outgoing.astype(BF16).reshape(experts, cap, feat)
    vmem = pl.BlockSpec(memory_space=pltpu.VMEM)
    hbm = pl.BlockSpec(memory_space=pl.ANY)
    dma = pltpu.SemaphoreType.DMA
    chips = depth // feat
    token_grad, gate_grad, up_grad = pl.pallas_call(
        kernel,
        out_shape=(
            jax.ShapeDtypeStruct((tok_dev, feat), BF16),
            jax.ShapeDtypeStruct((depth, hidden), BF16),
            jax.ShapeDtypeStruct((depth, hidden), BF16),
        ),
        in_specs=[vmem, hbm, hbm, vmem, vmem],
        out_specs=[vmem, hbm, hbm],
        scratch_shapes=[
            pltpu.VMEM((depth, 2 * hidden), BF16),
            pltpu.VMEM((experts, 2 * cap, depth), BF16),
            pltpu.VMEM((experts, 2 * cap, 2 * hidden), F32),
            pltpu.VMEM((experts, cap, 2 * hidden), BF16),
            pltpu.VMEM((experts, cap, 2 * hidden), BF16),
            pltpu.VMEM((experts, 2 * cap, 2 * hidden), BF16),
            pltpu.VMEM((experts, 2 * cap, depth), BF16),
            pltpu.VMEM((experts, 2 * cap, half * feat), BF16),
            pltpu.VMEM((experts, 2, half, cap, feat), BF16),
            pltpu.VMEM((experts, 2, half, cap, feat), BF16),
            pltpu.VMEM((2 * experts - 1, cap, feat), BF16),
            pltpu.VMEM((experts, cap, feat), BF16),
            pltpu.VMEM((depth, 2 * hidden), BF16),
            dma((2,)), dma((chips, 2)),
            dma, dma((experts, 2)),
            dma((2,)), dma((experts, 2, half)),
            dma, dma((experts,)),
            dma, dma((experts,)),
            dma, dma((experts,)),
            dma, dma((experts,)),
            dma, dma((experts, 2, half)),
            dma, dma((experts,)),
        ],
        compiler_params=pltpu.CompilerParams(
            collective_id=0, has_side_effects=True, vmem_limit_bytes=56 * 2**20
        ),
        cost_estimate=pl.CostEstimate(
            flops=3 * 2 * experts * 2 * cap * depth * 2 * hidden,
            bytes_accessed=8 * depth * hidden,
            transcendentals=experts * cap * hidden,
        ),
    )(outgoing, w_gate[0], w_up[0], slot_grad[0, 0], token_of)
    return token_grad, gate_grad[None], up_grad[None]


def solution(mesh):
    in_specs = (
        P(("dp", "expert"), "etp"),
        P(("dp", "expert"), None),
        P("expert", "dp", "etp"),
        P("expert", "dp", "etp"),
        P("dp", "expert", None, None, "etp"),
    )
    out_specs = (P(("dp", "expert"), "etp"), P("expert", "dp", "etp"), P("expert", "dp", "etp"))
    return jax.shard_map(local, mesh=mesh, in_specs=in_specs, out_specs=out_specs, check_vma=False)
```

time: 475 us -> 171 us (0.36)
  waiting for transfers between devices: 379 us -> 0 us
  Pallas kernels: 0 us -> 159 us
  blocking collectives: 31.7 us -> 0 us
  matrix products: 31.3 us -> 0.98 us
  between operations: 13.9 us -> 0.7 us
  other arithmetic: 8.28 us -> 1.53 us
    all_gather x2 -> x0, waiting for transfers between devices: 194 us -> none  [the longest x1 158 us: local(): full = lax.all_gather(joined, 'dp', axis=0, tiled=True)]
    reduce_scatter x2 -> x0, waiting for transfers between devices: 186 us -> none  [the longest x1 136 us: local(): lax.psum_scatter(lax.dot_general(x_rows, d_both, (((0,), (0,)), ((), ()))...]
    pallas_call x0 -> x1, Pallas kernels: none -> 159 us  [local(): pl.pallas_call(kernel, out_shape=(jax.ShapeDtypeStruct((tok_dev, feat), B...]
    all_to_all x2 -> x0, blocking collectives: 31.7 us -> none  [the longest x1 16.1 us: local(): lax.all_to_all(outgoing, 'expert', split_axis=0, concat_axis=0, tiled=True)]
    dot_general x4 -> x0, matrix products: 31 us -> none  [the longest x1 12.2 us: local(): lax.dot_general(x_rows, d_both, (((0,), (0,)), ((), ())), preferred_eleme...]
    unnamed x7 -> x10, local copies, waits for them, and re-layouts: 0.8 us -> 7.96 us
    concatenate x1 -> x0, other arithmetic: 6.33 us -> none  [local(): joined = jnp.concatenate((w_gate[0], w_up[0]), axis=1)]
    broadcast_in_dim x1 -> x0, local copies, waits for them, and re-layouts: 5.95 us -> none  [local(): up_grad = summed_weights[:, hidden:][None]]
  transfers between devices with their start and end apart: 4 -> 0, of which waited for: 4 -> 0; matrix products, arithmetic and copies ran while one was open for 4% -> 0% of each run, Pallas kernels for 0% -> 0%
where the time goes in v1:
time: 171 us
  Pallas kernels  159 us (93%)
  local copies, waits for them, and re-layouts  8.66 us (5%)
    pallas_call x1, Pallas kernels, local(): pl.pallas_call(kernel, out_shape=(jax.ShapeDtypeStruct((tok_dev, feat), B...  159 us
    unnamed x10, local copies, waits for them, and re-layouts  7.96 us

profile of v1, /device:TPU:32, one launch (start us, length us, event | category | flops | bytes accessed | tf_op | source)
XLA Modules:
  0.0 170.6 jit_solution(2312144612193973485)
XLA Ops:
  0.6 0.0 copy-start
  0.6 0.8 copy.18
  1.5 0.1 eq.43
  1.6 0.1 eq.39
  1.8 0.6 reduce-window.6
  2.3 0.2 slice_reduce_fusion
  2.6 0.1 fusion.3
  2.7 0.1 reduce_sum.24
  2.8 0.1 copy.20
  2.9 0.7 multiply_add_fusion
  3.6 0.1 fusion.1.token_of
  3.7 0.0 copy-done
  3.7 0.0 copy-start.2
  3.7 1.0 convolution_convert_fusion
  4.7 0.0 copy-done.2
  4.7 158.8 %shard_map.76 = (bf16[128,384]{1,0:T(8,128)(2,1)}, bf16[3072,512]{1,0:T(8,128)(2,1)}, bf16[3072,512]{1,0:T(8,128)(2,1)}) custom-call(bf16[8,48,384]{2,1,0:T(8,128)(2,1)} %bitcast.18, bf16[3072,512]{1,0:T(8,128)(2,1)} %bitcast.19, bf16[3072,512]{1,0:T(8,128)(2,1)} %bitcast.20, bf16[8,48,512]{2,1,0:T(8,128)(2,1)} %bitcast.21, bf16[128,384]{1,0:T(8,128)(2,1)} %copy-done.2), custom_call_target="tpu_custom_call" | custom-call | flops 14495514624 | bytes 12582912 | tf_op jit(solution)/shard_map/pallas_call | solution.py:352
  163.5 1.5 copy.24
  165.0 0.0 copy-start.1
  165.0 3.9 %copy.25 = bf16[1,3072,512]{2,1,0:T(8,128)(2,1)} copy(bf16[1,3072,512]{2,1,0:T(8,128)(2,1)} %bitcast.17) | data formatting | bytes 6291456
  169.0 0.0 copy-done.1
  169.0 1.7 copy.26
  (3 shorter events, 0.0 us)
Async XLA Ops:
  0.6 3.1 %copy-start = (bf16[128,384]{1,0:T(8,128)(2,1)S(1)}, bf16[128,384]{1,0:T(8,128)(2,1)}, u32[]{:S(2)}) copy-start(bf16[128,384]{1,0:T(8,128)(2,1)} %param.5) | copy-start | bytes 294916
  3.7 1.0 copy-start.2
  165.0 3.9 %copy-start.1 = (bf16[3072,512]{1,0:T(8,128)(2,1)S(1)}, bf16[3072,512]{1,0:T(8,128)(2,1)}, u32[]{:S(2)}) copy-start(bf16[3072,512]{1,0:T(8,128)(2,1)} %get-tuple-element.8) | copy-start | bytes 9437188

commit v2 on v1

v2 whole, which is shorter than its diff:
```python
import functools

import jax
import jax.numpy as jnp
from jax import lax
from jax.experimental import pallas as pl
from jax.experimental.pallas import tpu as pltpu
from jax.sharding import PartitionSpec as P

MESH = pl.DeviceIdType.MESH
F32 = jnp.float32
BF16 = jnp.bfloat16

LAG_ACT = 2
LAG_RS = 1


def tile_of(size, most):
    return most if size % most == 0 else size


def kernel(
    tokens, routes, w_gate, w_up, slot_grad,
    token_grad, gate_grad, up_grad,
    w_v, w_t, token_of, outgoing, rows, part, y_out, y_in, sg_v, d_v, g_v, g_in, rs_out, rs_in, fin, ret, dw_v,
    w_sem, dw_sem, disp_send, disp_recv, ag_send, ag_recv, sib_send, sib_recv,
    sg_send, sg_recv, y_send, y_recv, g_send, g_recv, rs_send, rs_recv, ret_send, ret_recv,
):
    experts, cap, feat = outgoing.shape
    tok_dev = tokens.shape[0]
    depth, hidden = w_gate.shape
    chips = depth // feat
    half = chips // 2
    r = lax.axis_index("dp")
    x = lax.axis_index("expert")
    m = lax.axis_index("etp")
    z = m // 2
    c = m % 2
    i_own = z % half
    across = (z + half) % chips
    h = z // half
    z_from = jnp.where(h == r, z, across)
    alone = jnp.logical_and(r == 0, h == 0)
    up = (r, x, ((z + 1) % chips) * 2 + c)
    down = (r, x, ((z + chips - 1) % chips) * 2 + c)

    def held(k, s):
        return jnp.where(s // half == r, k % 2, 1 - k % 2)

    def target(k):
        return (h, (x + experts - k) % experts, jnp.where(r == k % 2, z, across) * 2 + c)

    def origin(k):
        return (held(k, z), (x + k) % experts, z_from * 2 + c)

    sibling = (r, x, z * 2 + 1 - c)
    partner = (1 - r, x, m)

    def wait(ref, sem):
        pltpu.make_async_copy(ref, ref, sem).wait()

    def send(src, dst, send_sem, recv_sem, device):
        pltpu.make_async_remote_copy(
            src_ref=src, dst_ref=dst, send_sem=send_sem, recv_sem=recv_sem,
            device_id=device, device_id_type=MESH,
        ).start()

    barrier = pltpu.get_barrier_semaphore()

    def greet(k, carry):
        @pl.when(jnp.logical_not(jnp.logical_and(alone, k == 0)))
        def _():
            for device in (target(k), origin(k)):
                pl.semaphore_signal(barrier, inc=1, device_id=device, device_id_type=MESH)

        return carry

    lax.fori_loop(0, experts, greet, 0)
    for device in (up, down, sibling, partner):
        pl.semaphore_signal(barrier, inc=1, device_id=device, device_id_type=MESH)

    load_gate = pltpu.make_async_copy(w_gate, w_v.at[:, pl.ds(0, hidden)], w_sem.at[0])
    load_up = pltpu.make_async_copy(w_up, w_v.at[:, pl.ds(hidden, hidden)], w_sem.at[1])
    load_gate.start()
    load_up.start()
    keep_grad = pltpu.make_async_copy(slot_grad, sg_v.at[r], w_sem.at[2])
    keep_grad.start()

    slots = experts * cap
    place = lax.broadcasted_iota(jnp.int32, (slots, tok_dev), 0)
    expert_of = place // cap
    names = jnp.logical_or(routes[0:1, :] == expert_of, routes[1:2, :] == expert_of)
    earlier = (
        lax.broadcasted_iota(jnp.int32, (tok_dev, tok_dev), 0)
        < lax.broadcasted_iota(jnp.int32, (tok_dev, tok_dev), 1)
    )
    count = jnp.dot(
        names.astype(F32).astype(BF16), earlier.astype(F32).astype(BF16), preferred_element_type=F32
    )
    here = jnp.logical_and(names, count == (place - expert_of * cap).astype(F32))
    token_of[...] = here.astype(F32).astype(BF16)
    outgoing[...] = jnp.dot(
        token_of[...], tokens[...], preferred_element_type=F32
    ).astype(BF16).reshape(experts, cap, feat)

    @pl.when(alone)
    def _():
        pl.semaphore_wait(barrier, 2 * experts + 2)

    @pl.when(jnp.logical_not(alone))
    def _():
        pl.semaphore_wait(barrier, 2 * experts + 4)

    def feats(i, core):
        return pl.ds(pl.multiple_of((2 * i + core) * feat, 128), feat)

    def rows_of(which):
        return pl.ds(pl.multiple_of(which * cap, 16), cap)

    def block_at(k, s):
        return rows.at[k, rows_of(held(k, s)), feats(s % half, c)]

    def dispatch(k, carry):
        there = (x + experts - k) % experts
        dst = rows.at[k, rows_of(r), feats(i_own, c)]
        to_self = jnp.logical_and(alone, k == 0)

        @pl.when(to_self)
        def _():
            pltpu.make_async_copy(outgoing.at[there], dst, disp_recv.at[k]).start()

        @pl.when(jnp.logical_not(to_self))
        def _():
            send(outgoing.at[there], dst, disp_send, disp_recv.at[k], target(k))

        return carry

    lax.fori_loop(0, experts, dispatch, 0)
    send(slot_grad, sg_v.at[r], sg_send, sg_recv, partner)

    def on_ring(k, distance):
        return (z + chips + (1 - 2 * (k % 2)) * distance) % chips

    def beside(k, distance):
        return (r, x, on_ring(k, distance) * 2 + c)

    def gather_step(k, d):
        @pl.when(d == 0)
        def _():
            own = block_at(k, z)
            wait(own, disp_recv.at[k])
            send(own, own, ag_send, ag_recv.at[k, 0, 0], beside(k, 1))
            if half > 1:
                send(own, own, ag_send, ag_recv.at[k, 1, 0], beside(k, -1))
            send(own, own, sib_send, sib_recv.at[k], sibling)

        @pl.when(d > 0)
        def _():
            block = block_at(k, on_ring(k, -d))
            wait(block, ag_recv.at[k, 0, d - 1])

            @pl.when(d < half)
            def _():
                send(block, block, ag_send, ag_recv.at[k, 0, d], beside(k, 1))

            send(block, block, sib_send, sib_recv.at[k], sibling)

        @pl.when(jnp.logical_and(d > 0, d < half))
        def _():
            block = block_at(k, on_ring(k, d))
            wait(block, ag_recv.at[k, 1, d - 1])

            @pl.when(d < half - 1)
            def _():
                send(block, block, ag_send, ag_recv.at[k, 1, d], beside(k, -1))

            send(block, block, sib_send, sib_recv.at[k], sibling)

    def reduce_step(k, d):
        def term(s):
            which = rows_of(held(k, s))
            packed = pl.ds(pl.multiple_of((s % half) * feat, 128), feat)
            return g_v[k, which, feats(s % half, c)].astype(F32) + g_in[k, which, packed].astype(F32)

        @pl.when(d == 0)
        def _():
            wait(g_in.at[k], g_recv.at[k])
            rs_out[k, 0, 0] = term(on_ring(k, half)).astype(BF16)
            send(rs_out.at[k, 0, 0], rs_in.at[k, 0, 0], rs_send, rs_recv.at[k, 0, 0], beside(k, -1))

        @pl.when(jnp.logical_and(d > 0, d < half))
        def _():
            wait(rs_in.at[k, 0, d - 1], rs_recv.at[k, 0, d - 1])
            total = term(on_ring(k, d - half)) + rs_in[k, 0, d - 1].astype(F32)
            rs_out[k, 0, d] = total.astype(BF16)
            send(rs_out.at[k, 0, d], rs_in.at[k, 0, d], rs_send, rs_recv.at[k, 0, d], beside(k, -1))

        @pl.when(jnp.logical_and(d == 1, half > 1))
        def _():
            rs_out[k, 1, 1] = term(on_ring(k, half - 1)).astype(BF16)

        @pl.when(jnp.logical_and(d > 1, d < half))
        def _():
            wait(rs_in.at[k, 1, d - 1], rs_recv.at[k, 1, d - 1])
            total = term(on_ring(k, half - d)) + rs_in[k, 1, d - 1].astype(F32)
            rs_out[k, 1, d] = total.astype(BF16)

        @pl.when(jnp.logical_and(d > 0, d < half))
        def _():
            send(rs_out.at[k, 1, d], rs_in.at[k, 1, d], rs_send, rs_recv.at[k, 1, d], beside(k, 1))

        @pl.when(d == half)
        def _():
            wait(rs_in.at[k, 0, half - 1], rs_recv.at[k, 0, half - 1])
            total = term(z) + rs_in[k, 0, half - 1].astype(F32)
            if half > 1:
                wait(rs_in.at[k, 1, half - 1], rs_recv.at[k, 1, half - 1])
                total = total + rs_in[k, 1, half - 1].astype(F32)
            fin[k] = total.astype(BF16)
            to_self = jnp.logical_and(alone, k == 0)

            @pl.when(to_self)
            def _():
                pltpu.make_async_copy(fin.at[k], ret.at[x], ret_recv.at[x]).start()

            @pl.when(jnp.logical_not(to_self))
            def _():
                send(fin.at[k], ret.at[x], ret_send, ret_recv.at[x], origin(k))

    wide = 2 * hidden
    fwd_tile = tile_of(wide, 512)
    dx_tile = tile_of(depth, 1024)

    load_gate.wait()
    load_up.wait()

    def turn(j, carry):
        columns = pl.ds(pl.multiple_of(j * dx_tile, 128), dx_tile)
        w_t[:, columns] = w_v[columns, :].T
        return carry

    lax.fori_loop(0, depth // dx_tile, turn, 0)

    def forward(k):
        wait(rows.at[k, :, pl.ds(0, half * feat)], sib_recv.at[k])

        def tile(j, carry):
            columns = pl.ds(pl.multiple_of(j * fwd_tile, 128), fwd_tile)
            product = jnp.dot(rows[k], w_v[:, columns], preferred_element_type=F32)
            part[k, :, columns] = product
            y_out[k, :, columns] = product.astype(BF16)
            return carry

        lax.fori_loop(0, wide // fwd_tile, tile, 0)
        send(y_out.at[k], y_in.at[k], y_send, y_recv.at[k], partner)

    def backward(k):
        @pl.when(k == 0)
        def _():
            keep_grad.wait()
            wait(sg_v.at[1 - r], sg_recv)

        wait(y_in.at[k], y_recv.at[k])
        source = (x + k) % experts
        for which in range(2):
            mine = pl.ds(which * cap, cap)
            gate = part[k, mine, pl.ds(0, hidden)] + y_in[k, mine, pl.ds(0, hidden)].astype(F32)
            up_v = part[k, mine, pl.ds(hidden, hidden)] + y_in[k, mine, pl.ds(hidden, hidden)].astype(F32)
            sig = jax.nn.sigmoid(gate)
            gs = sg_v[which, source].astype(F32) * sig
            d_v[k, mine, pl.ds(0, hidden)] = (gs * up_v * (1.0 + gate * (1.0 - sig))).astype(BF16)
            d_v[k, mine, pl.ds(hidden, hidden)] = (gs * gate).astype(BF16)

        def tile(j, carry):
            columns = pl.ds(pl.multiple_of(j * dx_tile, 128), dx_tile)
            g_v[k, :, columns] = jnp.dot(
                d_v[k], w_t[:, columns], preferred_element_type=F32
            ).astype(BF16)
            return carry

        lax.fori_loop(0, depth // dx_tile, tile, 0)
        for i in range(half):
            send(
                g_v.at[k, :, feats(i, 1 - c)], g_in.at[k, :, pl.ds(i * feat, feat)],
                g_send, g_recv.at[k], sibling,
            )

    dw_tile = tile_of(hidden, 256)

    def weight_piece(p):
        here = pl.ds(pl.multiple_of(p * feat, 128), feat)
        block = rows[:, :, here].reshape(experts * 2 * cap, feat)

        def tile(j, carry):
            columns = pl.ds(pl.multiple_of(j * dw_tile, 128), dw_tile)
            dw_v[here, columns] = lax.dot_general(
                block, d_v[:, :, columns].reshape(experts * 2 * cap, dw_tile),
                (((0,), (0,)), ((), ())), preferred_element_type=F32,
            ).astype(BF16)
            return carry

        lax.fori_loop(0, wide // dw_tile, tile, 0)
        pltpu.make_async_copy(
            dw_v.at[here, pl.ds(0, hidden)], gate_grad.at[here, :], dw_sem.at[p, 0]
        ).start()
        pltpu.make_async_copy(
            dw_v.at[here, pl.ds(hidden, hidden)], up_grad.at[here, :], dw_sem.at[p, 1]
        ).start()

    at_fwd = half + 1
    at_act = at_fwd + LAG_ACT
    at_rs = at_act + LAG_RS
    last = experts - 1
    ticks = last + at_rs + half + 1
    at_dw = last + at_act + 1
    per_tick = -(-chips // half)

    def tick(t, carry):
        def transfers(k, inner):
            u = t - k
            d = u - at_rs

            @pl.when(jnp.logical_and(d >= 0, d <= half))
            def _():
                reduce_step(k, d)

            @pl.when(jnp.logical_and(u >= 0, u <= half))
            def _():
                gather_step(k, u)

            return inner

        lax.fori_loop(0, experts, transfers, 0)

        def work(k, inner):
            u = t - k
            pl.when(u == at_act)(functools.partial(backward, k))
            pl.when(u == at_fwd)(functools.partial(forward, k))
            return inner

        lax.fori_loop(0, experts, work, 0)

        def pieces(q, inner):
            p = (t - at_dw) * per_tick + q
            pl.when(jnp.logical_and(p >= 0, p < chips))(functools.partial(weight_piece, p))
            return inner

        lax.fori_loop(0, per_tick, pieces, 0)
        return carry

    lax.fori_loop(0, ticks, tick, 0)

    def returned(k, carry):
        wait(ret.at[k], ret_recv.at[k])
        return carry

    lax.fori_loop(0, experts, returned, 0)
    token_grad[...] = lax.dot_general(
        token_of[...], ret[...].reshape(slots, feat), (((0,), (0,)), ((), ())), preferred_element_type=F32
    ).astype(BF16)

    @pl.when(alone)
    def _():
        wait(outgoing.at[pl.ds(0, experts - 1)], disp_send)
        wait(fin.at[pl.ds(0, experts - 1)], ret_send)

    @pl.when(jnp.logical_not(alone))
    def _():
        wait(outgoing, disp_send)
        wait(fin, ret_send)

    wait(slot_grad, sg_send)
    wait(rows.at[:, pl.ds(0, cap), pl.ds(0, (chips - 1) * feat)], ag_send)
    wait(rows.at[:, :, pl.ds(0, half * feat)], sib_send)
    wait(y_out, y_send)
    wait(g_in, g_send)
    wait(rows.at[:, pl.ds(0, cap), pl.ds(0, (chips - 1) * feat)], rs_send)

    def written(p, carry):
        here = pl.ds(pl.multiple_of(p * feat, 128), feat)
        wait(dw_v.at[here, pl.ds(0, hidden)], dw_sem.at[p, 0])
        wait(dw_v.at[here, pl.ds(hidden, hidden)], dw_sem.at[p, 1])
        return carry

    lax.fori_loop(0, chips, written, 0)


def local(tokens, routes, w_gate, w_up, slot_grad):
    tok_dev, feat = tokens.shape
    experts = lax.axis_size("expert")
    cap = slot_grad.shape[3]
    _, depth, hidden = w_gate.shape
    chips = depth // feat
    half = chips // 2
    vmem = pl.BlockSpec(memory_space=pltpu.VMEM)
    hbm = pl.BlockSpec(memory_space=pl.ANY)
    dma = pltpu.SemaphoreType.DMA
    token_grad, gate_grad, up_grad = pl.pallas_call(
        kernel,
        out_shape=(
            jax.ShapeDtypeStruct((tok_dev, feat), BF16),
            jax.ShapeDtypeStruct((depth, hidden), BF16),
            jax.ShapeDtypeStruct((depth, hidden), BF16),
        ),
        in_specs=[vmem, vmem, hbm, hbm, vmem],
        out_specs=[vmem, hbm, hbm],
        scratch_shapes=[
            pltpu.VMEM((depth, 2 * hidden), BF16),
            pltpu.VMEM((2 * hidden, depth), BF16),
            pltpu.VMEM((experts * cap, tok_dev), BF16),
            pltpu.VMEM((experts, cap, feat), BF16),
            pltpu.VMEM((experts, 2 * cap, depth), BF16),
            pltpu.VMEM((experts, 2 * cap, 2 * hidden), F32),
            pltpu.VMEM((experts, 2 * cap, 2 * hidden), BF16),
            pltpu.VMEM((experts, 2 * cap, 2 * hidden), BF16),
            pltpu.VMEM((2, experts, cap, hidden), BF16),
            pltpu.VMEM((experts, 2 * cap, 2 * hidden), BF16),
            pltpu.VMEM((experts, 2 * cap, depth), BF16),
            pltpu.VMEM((experts, 2 * cap, half * feat), BF16),
            pltpu.VMEM((experts, 2, half, cap, feat), BF16),
            pltpu.VMEM((experts, 2, half, cap, feat), BF16),
            pltpu.VMEM((experts, cap, feat), BF16),
            pltpu.VMEM((experts, cap, feat), BF16),
            pltpu.VMEM((depth, 2 * hidden), BF16),
            dma((3,)), dma((chips, 2)),
            dma, dma((experts,)),
            dma, dma((experts, 2, half)),
            dma, dma((experts,)),
            dma, dma,
            dma, dma((experts,)),
            dma, dma((experts,)),
            dma, dma((experts, 2, half)),
            dma, dma((experts,)),
        ],
        compiler_params=pltpu.CompilerParams(
            collective_id=0, has_side_effects=True, vmem_limit_bytes=56 * 2**20
        ),
        cost_estimate=pl.CostEstimate(
            flops=3 * 2 * experts * 2 * cap * depth * 2 * hidden,
            bytes_accessed=8 * depth * hidden,
            transcendentals=experts * 2 * cap * hidden,
        ),
    )(tokens, routes.T, w_gate[0], w_up[0], slot_grad[0, 0])
    return token_grad, gate_grad[None], up_grad[None]


def solution(mesh):
    in_specs = (
        P(("dp", "expert"), "etp"),
        P(("dp", "expert"), None),
        P("expert", "dp", "etp"),
        P("expert", "dp", "etp"),
        P("dp", "expert", None, None, "etp"),
    )
    out_specs = (P(("dp", "expert"), "etp"), P("expert", "dp", "etp"), P("expert", "dp", "etp"))
    return jax.shard_map(local, mesh=mesh, in_specs=in_specs, out_specs=out_specs, check_vma=False)
```

time: 171 us -> 118 us (0.69)
  Pallas kernels: 159 us -> 110 us
    pallas_call x1, Pallas kernels: 159 us -> 110 us  [local(): pl.pallas_call(kernel, out_shape=(jax.ShapeDtypeStruct((tok_dev, feat), B...]
    unnamed x10 -> x5, local copies, waits for them, and re-layouts: 7.96 us -> 7.12 us
where the time goes in v2:
time: 118 us
  Pallas kernels  110 us (93%)
  local copies, waits for them, and re-layouts  7.12 us (6%)
    pallas_call x1, Pallas kernels, local(): pl.pallas_call(kernel, out_shape=(jax.ShapeDtypeStruct((tok_dev, feat), B...  110 us
    unnamed x5, local copies, waits for them, and re-layouts  7.12 us

profile of v2, /device:TPU:32, one launch (start us, length us, event | category | flops | bytes accessed | tf_op | source)
XLA Modules:
  0.0 117.8 jit_solution(11812783910893024977)
XLA Ops:
  0.6 110.0 %shard_map.76 = (bf16[128,384]{1,0:T(8,128)(2,1)}, bf16[3072,512]{1,0:T(8,128)(2,1)}, bf16[3072,512]{1,0:T(8,128)(2,1)}) custom-call(bf16[128,384]{1,0:T(8,128)(2,1)} %tokens.1, s32[2,128]{1,0:T(2,128)} %bitcast.11, bf16[3072,512]{1,0:T(8,128)(2,1)} %bitcast.8, bf16[3072,512]{1,0:T(8,128)(2,1)} %bitcast.9, bf16[8,48,512]{2,1,0:T(8,128)(2,1)} %bitcast.10), custom_call_target="tpu_custom_call" | custom-call | flops 14495514624 | bytes 12582912 | tf_op jit(solution)/shard_map/pallas_call | solution.py:398
  110.7 1.5 %copy.11 = bf16[128,384]{1,0:T(8,128)(2,1)} copy(bf16[128,384]{1,0:T(8,128)(2,1)} %get-tuple-element.12) | data formatting | bytes 196608
  112.2 0.0 copy-start
  112.2 3.9 %copy.12 = bf16[1,3072,512]{2,1,0:T(8,128)(2,1)} copy(bf16[1,3072,512]{2,1,0:T(8,128)(2,1)} %bitcast.7) | data formatting | bytes 6291456
  116.1 0.0 copy-done
  116.1 1.7 %copy.13 = bf16[1,3072,512]{2,1,0:T(8,128)(2,1)} copy(bf16[1,3072,512]{2,1,0:T(8,128)(2,1)S(1)} %bitcast.6) | data formatting | bytes 6291456
Async XLA Ops:
  112.2 3.9 %copy-start = (bf16[3072,512]{1,0:T(8,128)(2,1)S(1)}, bf16[3072,512]{1,0:T(8,128)(2,1)}, u32[]{:S(2)}) copy-start(bf16[3072,512]{1,0:T(8,128)(2,1)} %get-tuple-element.8) | copy-start | bytes 9437188

commit v3 on v2

--- a/solution.py
+++ b/solution.py
@@ -21,7 +21,7 @@
 
 def kernel(
     tokens, routes, w_gate, w_up, slot_grad,
-    token_grad, gate_grad, up_grad,
+    token_grad, weight_grads,
     w_v, w_t, token_of, outgoing, rows, part, y_out, y_in, sg_v, d_v, g_v, g_in, rs_out, rs_in, fin, ret, dw_v,
     w_sem, dw_sem, disp_send, disp_recv, ag_send, ag_recv, sib_send, sib_recv,
     sg_send, sg_recv, y_send, y_recv, g_send, g_recv, rs_send, rs_recv, ret_send, ret_recv,
@@ -37,12 +37,15 @@
     z = m // 2
     c = m % 2
     i_own = z % half
-    across = (z + half) % chips
+    across = chips - 1 - z
     h = z // half
     z_from = jnp.where(h == r, z, across)
     alone = jnp.logical_and(r == 0, h == 0)
     up = (r, x, ((z + 1) % chips) * 2 + c)
     down = (r, x, ((z + chips - 1) % chips) * 2 + c)
+
+    def feature(s):
+        return jnp.where(s // half == r, s % half, half - 1 - s % half)
 
     def held(k, s):
         return jnp.where(s // half == r, k % 2, 1 - k % 2)
@@ -118,7 +121,7 @@
         return pl.ds(pl.multiple_of(which * cap, 16), cap)
 
     def block_at(k, s):
-        return rows.at[k, rows_of(held(k, s)), feats(s % half, c)]
+        return rows.at[k, rows_of(held(k, s)), feats(feature(s), c)]
 
     def dispatch(k, carry):
         there = (x + experts - k) % experts
@@ -179,8 +182,8 @@
     def reduce_step(k, d):
         def term(s):
             which = rows_of(held(k, s))
-            packed = pl.ds(pl.multiple_of((s % half) * feat, 128), feat)
-            return g_v[k, which, feats(s % half, c)].astype(F32) + g_in[k, which, packed].astype(F32)
+            packed = pl.ds(pl.multiple_of(feature(s) * feat, 128), feat)
+            return g_v[k, which, feats(feature(s), c)].astype(F32) + g_in[k, which, packed].astype(F32)
 
         @pl.when(d == 0)
         def _():
@@ -301,10 +304,10 @@
 
         lax.fori_loop(0, wide // dw_tile, tile, 0)
         pltpu.make_async_copy(
-            dw_v.at[here, pl.ds(0, hidden)], gate_grad.at[here, :], dw_sem.at[p, 0]
+            dw_v.at[here, pl.ds(0, hidden)], weight_grads.at[0, here, :], dw_sem.at[p, 0]
         ).start()
         pltpu.make_async_copy(
-            dw_v.at[here, pl.ds(hidden, hidden)], up_grad.at[here, :], dw_sem.at[p, 1]
+            dw_v.at[here, pl.ds(hidden, hidden)], weight_grads.at[1, here, :], dw_sem.at[p, 1]
         ).start()
 
     at_fwd = half + 1
@@ -395,15 +398,14 @@
     vmem = pl.BlockSpec(memory_space=pltpu.VMEM)
     hbm = pl.BlockSpec(memory_space=pl.ANY)
     dma = pltpu.SemaphoreType.DMA
-    token_grad, gate_grad, up_grad = pl.pallas_call(
+    token_grad, weight_grads = pl.pallas_call(
         kernel,
         out_shape=(
             jax.ShapeDtypeStruct((tok_dev, feat), BF16),
-            jax.ShapeDtypeStruct((depth, hidden), BF16),
-            jax.ShapeDtypeStruct((depth, hidden), BF16),
+            jax.ShapeDtypeStruct((2, depth, hidden), BF16),
         ),
         in_specs=[vmem, vmem, hbm, hbm, vmem],
-        out_specs=[vmem, hbm, hbm],
+        out_specs=[vmem, hbm],
         scratch_shapes=[
             pltpu.VMEM((depth, 2 * hidden), BF16),
             pltpu.VMEM((2 * hidden, depth), BF16),
@@ -441,7 +443,7 @@
             transcendentals=experts * 2 * cap * hidden,
         ),
     )(tokens, routes.T, w_gate[0], w_up[0], slot_grad[0, 0])
-    return token_grad, gate_grad[None], up_grad[None]
+    return token_grad, weight_grads[0:1], weight_grads[1:2]
 
 
 def solution(mesh):

time: 118 us -> 114 us (0.966)
  Pallas kernels: 110 us -> 105 us
    unnamed x5 -> x3, local copies, waits for them, and re-layouts: 7.12 us -> 0.64 us
    slice x0 -> x1, local copies, waits for them, and re-layouts: none -> 5.98 us  [local(): return (token_grad, weight_grads[0:1], weight_grads[1:2])]
    pallas_call x1, Pallas kernels: 110 us -> 105 us  [local(): pl.pallas_call(kernel, out_shape=(jax.ShapeDtypeStruct((tok_dev, feat), B...]
where the time goes in v3:
time: 114 us; the launch traced here: 113 us
  Pallas kernels  105 us (92%)
  local copies, waits for them, and re-layouts  6.62 us (6%)
    pallas_call x1, Pallas kernels, local(): pl.pallas_call(kernel, out_shape=(jax.ShapeDtypeStruct((tok_dev, feat), B...  105 us
    slice x1, local copies, waits for them, and re-layouts, local(): return (token_grad, weight_grads[0:1], weight_grads[1:2])  5.98 us

profile of v3, /device:TPU:32, one launch (start us, length us, event | category | flops | bytes accessed | tf_op | source)
XLA Modules:
  0.0 112.8 jit_solution(2684397906463782481)
XLA Ops:
  0.6 105.5 %shard_map.76 = (bf16[128,384]{1,0:T(8,128)(2,1)}, bf16[2,3072,512]{2,1,0:T(8,128)(2,1)}) custom-call(bf16[128,384]{1,0:T(8,128)(2,1)} %tokens.1, s32[2,128]{1,0:T(2,128)} %bitcast.7, bf16[3072,512]{1,0:T(8,128)(2,1)} %bitcast.4, bf16[3072,512]{1,0:T(8,128)(2,1)} %bitcast.5, bf16[8,48,512]{2,1,0:T(8,128)(2,1)} %bitcast.6), custom_call_target="tpu_custom_call" | custom-call | flops 14495514624 | bytes 12582912 | tf_op jit(solution)/shard_map/pallas_call | solution.py:401
  106.1 0.0 copy-start
  106.1 6.0 %fusion = (bf16[1,3072,512]{2,1,0:T(8,128)(2,1)}, bf16[1,3072,512]{2,1,0:T(8,128)(2,1)}) fusion(bf16[2,3072,512]{2,1,0:T(8,128)(2,1)} %get-tuple-element.6), kind=kLoop, calls=%fused_computation | loop fusion | bytes 12582912 | tf_op jit(solution)/shard_map/slice | solution.py:446
  112.1 0.0 copy-done
  112.1 0.6 copy.9
Async XLA Ops:
  106.1 6.0 %copy-start = (bf16[128,384]{1,0:T(8,128)(2,1)S(1)}, bf16[128,384]{1,0:T(8,128)(2,1)}, u32[]{:S(2)}) copy-start(bf16[128,384]{1,0:T(8,128)(2,1)} %get-tuple-element.12) | copy-start | bytes 294916

commit v4 on v3

--- a/solution.py
+++ b/solution.py
@@ -13,6 +13,7 @@
 
 LAG_ACT = 2
 LAG_RS = 1
+GRAD_TICK = 1
 
 
 def tile_of(size, most):
@@ -139,7 +140,6 @@
         return carry
 
     lax.fori_loop(0, experts, dispatch, 0)
-    send(slot_grad, sg_v.at[r], sg_send, sg_recv, partner)
 
     def on_ring(k, distance):
         return (z + chips + (1 - 2 * (k % 2)) * distance) % chips
@@ -252,10 +252,10 @@
             product = jnp.dot(rows[k], w_v[:, columns], preferred_element_type=F32)
             part[k, :, columns] = product
             y_out[k, :, columns] = product.astype(BF16)
+            send(y_out.at[k, :, columns], y_in.at[k, :, columns], y_send, y_recv.at[k], partner)
             return carry
 
         lax.fori_loop(0, wide // fwd_tile, tile, 0)
-        send(y_out.at[k], y_in.at[k], y_send, y_recv.at[k], partner)
 
     def backward(k):
         @pl.when(k == 0)
@@ -319,6 +319,10 @@
     per_tick = -(-chips // half)
 
     def tick(t, carry):
+        @pl.when(t == GRAD_TICK)
+        def _():
+            send(slot_grad, sg_v.at[r], sg_send, sg_recv, partner)
+
         def transfers(k, inner):
             u = t - k
             d = u - at_rs

time: 114 us -> 115 us (level)
  Pallas kernels: 105 us -> 107 us
    pallas_call x1, Pallas kernels: 105 us -> 107 us  [local(): pl.pallas_call(kernel, out_shape=(jax.ShapeDtypeStruct((tok_dev, feat), B...]
where the time goes in v4:
time: 115 us; the launch traced here: 114 us
  Pallas kernels  107 us (93%)
  local copies, waits for them, and re-layouts  6.62 us (6%)
    pallas_call x1, Pallas kernels, local(): pl.pallas_call(kernel, out_shape=(jax.ShapeDtypeStruct((tok_dev, feat), B...  107 us
    slice x1, local copies, waits for them, and re-layouts, local(): return (token_grad, weight_grads[0:1], weight_grads[1:2])  5.98 us

profile of v4, /device:TPU:32, one launch (start us, length us, event | category | flops | bytes accessed | tf_op | source)
XLA Modules:
  0.0 114.5 jit_solution(5419817828147016370)
XLA Ops:
  0.6 107.2 %shard_map.76 = (bf16[128,384]{1,0:T(8,128)(2,1)}, bf16[2,3072,512]{2,1,0:T(8,128)(2,1)}) custom-call(bf16[128,384]{1,0:T(8,128)(2,1)} %tokens.1, s32[2,128]{1,0:T(2,128)} %bitcast.7, bf16[3072,512]{1,0:T(8,128)(2,1)} %bitcast.4, bf16[3072,512]{1,0:T(8,128)(2,1)} %bitcast.5, bf16[8,48,512]{2,1,0:T(8,128)(2,1)} %bitcast.6), custom_call_target="tpu_custom_call" | custom-call | flops 14495514624 | bytes 12582912 | tf_op jit(solution)/shard_map/pallas_call | solution.py:405
  107.9 0.0 copy-start
  107.9 6.0 %fusion = (bf16[1,3072,512]{2,1,0:T(8,128)(2,1)}, bf16[1,3072,512]{2,1,0:T(8,128)(2,1)}) fusion(bf16[2,3072,512]{2,1,0:T(8,128)(2,1)} %get-tuple-element.6), kind=kLoop, calls=%fused_computation | loop fusion | bytes 12582912 | tf_op jit(solution)/shard_map/slice | solution.py:450
  113.9 0.0 copy-done
  113.9 0.6 copy.9
Async XLA Ops:
  107.9 6.0 %copy-start = (bf16[128,384]{1,0:T(8,128)(2,1)S(1)}, bf16[128,384]{1,0:T(8,128)(2,1)}, u32[]{:S(2)}) copy-start(bf16[128,384]{1,0:T(8,128)(2,1)} %get-tuple-element.12) | copy-start | bytes 294916
